TPU v7x, 32 devices: a whole 2x2x4 slice. The times are simulated.
32 devices in a mesh: groups: 2 (over y), sec: 4 (over z), strip: 4 (over x, core).
Axes of the slice: x: 2, y: 2, z: 4, core: 2. Of those that a mesh axis runs over, the one named last changes fastest.
Arguments:
- sections: bfloat16 [4, 256, 1024], P('sec', 'strip', 'groups'), parts along dimension 2, may hold values from -40 to 40
- mask_fine: int32 [4, 8, 32], P('sec', 'strip', 'groups'), parts along dimension 2, may hold values 0 or 1
- mask_coarse: int32 [4, 4, 16], P('sec', 'strip', 'groups'), parts along dimension 2, may hold values 0 or 1
Outputs:
- corr_fine: float32 [4, 2, 8, 32, 1024], P('sec', None, 'strip', 'groups'), parts along dimension 3
- corr_coarse: float32 [4, 2, 4, 16, 1024], P('sec', None, 'strip', 'groups'), parts along dimension 3
There are 2 independent parts, one for each index of `groups`. A program takes and returns all parts, laid end to end along the dimension named above; each array names one. Nothing has to cross between parts.
All inputs are finite; a program needn't handle non-finite values. No bound on the sum of `mask_fine` or of `mask_coarse` on one device may be relied on, other than what follows from the above.
Results may differ from a plain program's by a relative error of at most 0.0039.
Values may be sent and summed in bfloat16 or wider, within the bound.
No kernel may reach another device: no remote copies, remote signals or barrier semaphores. Data moves between devices by JAX's collectives and lax.ppermute only.
A program may use at most 64 MiB of HBM per device.

v0:
```python
import functools

import jax
import jax.numpy as jnp
import numpy as np
from jax import lax
from jax.experimental import pallas as pl
from jax.experimental.pallas import tpu as pltpu
from jax.sharding import PartitionSpec as P

PATCH = 64
STRIDE = 32
WINDOW = 32
HALF = PATCH // 2
LANES = 128
NYQ = 16

f32 = jnp.float32
bf16 = jnp.bfloat16


def shifted(value, axis, steps):
    count = lax.axis_size(axis)
    leading, last = (max(0, -steps), min(count, count - steps))
    return lax.ppermute(value, axis, [(source, source + steps) for source in range(leading, last)])


def wave(phase):
    turns = np.arange(PATCH) * (2 * np.pi / PATCH)
    cos = np.round(np.cos(turns), 14)
    sin = np.round(np.sin(turns), 14)
    phase = np.mod(phase, PATCH)
    return cos[phase], sin[phase]


def split_table(table):
    high = table.astype(jnp.bfloat16)
    low = (table - high.astype(np.float64)).astype(jnp.bfloat16)
    return high, low


def row_table(strip_rows):
    ext = strip_rows + PATCH
    fine, coarse = strip_rows // STRIDE, strip_rows // (2 * STRIDE)
    k = np.arange(HALF)[:, None]
    cos_rows, sin_rows, nyquist = [], [], np.zeros((NYQ, ext))
    for block in range(fine + coarse):
        cos = np.zeros((HALF, ext))
        sin = np.zeros((HALF, ext))
        if block < fine:
            x, first, scale = np.arange(PATCH), block * STRIDE, 1.0
        else:
            x, first, scale = np.arange(2 * PATCH) // 2, (block - fine) * 2 * STRIDE, 0.5
        c, s = wave(k * x[None, :])
        cos[:, first : first + x.size] = c * scale
        sin[:, first : first + x.size] = s * scale
        nyquist[block, first : first + x.size] = wave(HALF * x)[0] * scale
        cos_rows.append(cos)
        sin_rows.append(sin)
    table = np.concatenate(
        cos_rows[:fine] + [nyquist] + cos_rows[fine:] + sin_rows[:fine] + [np.zeros((NYQ, ext))] + sin_rows[fine:]
    )
    high, low = split_table(table)
    return np.concatenate([high, low], axis=1)


def stacked(table):
    high, low = split_table(table)
    return np.concatenate([high, high, low], axis=0)


def fine_table():
    c, s = wave(np.arange(PATCH)[:, None] * np.arange(PATCH)[None, :])
    table = np.zeros((2, 2, PATCH, 2, 2, PATCH))
    for p in range(2):
        table[0, p, :, 0, p] = c
        table[1, p, :, 0, p] = -s
        table[0, p, :, 1, p] = -s
        table[1, p, :, 1, p] = -c
    return stacked(table.reshape(4 * PATCH, 4 * PATCH))


def coarse_table():
    c, s = wave((np.arange(2 * PATCH) // 2)[:, None] * np.arange(PATCH)[None, :])
    table = np.zeros((2, 2, 2 * PATCH, 2, 2, PATCH))
    for p in range(2):
        table[p, 0, :, 0, p] = 0.5 * c
        table[p, 1, :, 0, p] = -0.5 * s
        table[p, 0, :, 1, p] = -0.5 * s
        table[p, 1, :, 1, p] = -0.5 * c
    return stacked(table.reshape(8 * PATCH, 4 * PATCH))


def shift_table():
    t = np.arange(WINDOW) - WINDOW // 2
    c, s = wave(np.arange(PATCH)[:, None] * t[None, :])
    table = np.zeros((2, 2, 2, PATCH, 2, 4, WINDOW))
    for odd in range(2):
        for p in range(2):
            table[odd, 0, p, :, 0, 2 * p + odd] = c
            table[odd, 1, p, :, 0, 2 * p + odd] = -s
            table[odd, 0, p, :, 1, 2 * p + odd] = s
            table[odd, 1, p, :, 1, 2 * p + odd] = c
    return stacked(table.reshape(8 * PATCH, 8 * WINDOW))


def map_table(blocks):
    shift = np.arange(WINDOW) - WINDOW // 2
    c, s = wave(shift[:, None] * np.arange(HALF)[None, :])
    weight = np.where(np.arange(HALF) == 0, 1.0, 2.0) / PATCH**3
    rows = []
    for block in range(blocks):
        nyquist = np.zeros((WINDOW, NYQ))
        nyquist[:, block] = wave(HALF * shift)[0] / PATCH**3
        high, low = split_table(np.concatenate([c * weight, -s * weight, nyquist], axis=1))
        top = np.concatenate([high, high], axis=1)
        bottom = np.concatenate([low, np.zeros_like(low)], axis=1)
        rows.append(np.concatenate([top, bottom], axis=0))
    return np.stack(rows)


def split(value):
    high = value.astype(bf16)
    return high, (value - high.astype(f32)).astype(bf16)


def dot(left, right):
    return jnp.dot(left, right, preferred_element_type=f32)


def dot3(value, table_ref):
    high, low = split(value)
    return dot(jnp.concatenate([high, low, high], axis=1), table_ref[...])


def kernel(
    fine, coarse, quads_fine, quads_coarse,
    own, rim, near, rim_near, far, rim_far, mask_ref,
    row_ref, fine_ref, coarse_ref, shift_ref, map_ref,
    out_fine, out_coarse,
    t_ref, spec_fine, spec_coarse, maps_ref,
):
    width = own.shape[1]
    fine_rows = fine * HALF
    fine_all = fine_rows + NYQ
    coarse_rows = coarse * HALF
    half_rows = fine_all + coarse_rows
    sub = lax.broadcasted_iota(jnp.int32, (8, LANES), 0)
    lane = lax.broadcasted_iota(jnp.int32, (8, LANES), 1)
    dc = (sub == 0) & (lane % PATCH == 0)
    group = lax.broadcasted_iota(jnp.int32, (LANES, LANES), 0) // PATCH
    same = group == lax.broadcasted_iota(jnp.int32, (LANES, LANES), 1) // PATCH
    ones = jnp.where(same, 1.0, 0.0).astype(bf16)
    ones = jnp.concatenate([ones, ones], axis=0)

    for z, (top, bottom) in enumerate(((own, rim), (near, rim_near), (far, rim_far))):
        x = jnp.concatenate([top[...], bottom[...]], axis=0)
        t = dot(row_ref[...], jnp.concatenate([x, x], axis=0))
        t_ref[z, :, :width] = t
        t_ref[z, :, width:] = jnp.zeros((2 * half_rows, LANES), f32)

    def power(values, first, nyquist_row):
        re, im = values[:, :LANES], values[:, LANES:]
        q = re * re + im * im
        total = None
        for r in range(0, HALF, 8):
            part = q[first + r : first + r + 8]
            if r == 0:
                part = jnp.where(dc, 0.0, part)
                head = jnp.where(sub == 0, part, 0.0)
            total = part if total is None else total + part
        tail = q[nyquist_row[0] : nyquist_row[0] + 8]
        return 2.0 * total - head + jnp.where(sub == nyquist_row[1], tail, 0.0)

    def normalise(spec_ref, z, tiles, blocks, block_first, nyquist_first, first_block, first_mask):
        rows = len(blocks)
        sums = []
        for tile in range(tiles):
            values = spec_ref[z, tile]
            for b in range(rows):
                sums.append(power(values, block_first + b * HALF, (nyquist_first, first_block + b)))
        stack = jnp.concatenate(sums, axis=0)
        high, low = split(stack)
        stack = dot(jnp.concatenate([high, low], axis=1), ones)
        for tile in range(tiles):
            values = spec_ref[z, tile]
            scales = []
            for b in range(rows):
                at = (tile * rows + b) * 8
                total = jnp.sum(stack[at : at + 8], axis=0, keepdims=True)
                scale = 1.0 / jnp.sqrt(total * (1.0 / PATCH**4) + 1e-05)
                if z == 0:
                    m = first_mask + tile * rows + b
                    scale = scale * mask_ref[m : m + 1, :]
                scales.append(jnp.concatenate([scale, scale], axis=1))
            parts = {}
            for b in range(rows):
                first = block_first + b * HALF
                block = values[first : first + HALF]
                head = jnp.where(jnp.concatenate([dc, dc], axis=1), 0.0, block[:8])
                block = jnp.concatenate([head, block[8:]], axis=0)
                parts[first] = block * scales[b]
            nyq = values[nyquist_first : nyquist_first + NYQ]
            row = lax.broadcasted_iota(jnp.int32, (NYQ, 2 * LANES), 0)
            scaled = jnp.zeros_like(nyq)
            for b in range(rows):
                scaled = jnp.where(row == first_block + b, nyq * scales[b], scaled)
            parts[nyquist_first] = scaled
            result = jnp.concatenate([parts[first] for first in sorted(parts)], axis=0)
            spec_ref[z, tile] = result.astype(bf16).astype(f32)

    for z in range(3):
        for m in range(quads_fine):
            for odd in range(2):
                at = LANES * m + STRIDE * odd
                value = jnp.concatenate(
                    [t_ref[z, :fine_all, at : at + LANES],
                     t_ref[z, half_rows : half_rows + fine_all, at : at + LANES]], axis=1)
                spec_fine[z, 2 * m + odd] = dot3(value, fine_ref)
        for n in range(quads_coarse):
            for odd in range(2):
                pieces = []
                for p in range(2):
                    at = 2 * LANES * n + LANES * p + 2 * STRIDE * odd
                    pieces += [t_ref[z, fine_rows:half_rows, at : at + LANES],
                               t_ref[z, half_rows + fine_rows : 2 * half_rows, at : at + LANES]]
                spec_coarse[z, 2 * n + odd] = dot3(jnp.concatenate(pieces, axis=1), coarse_ref)
        normalise(spec_fine, z, 2 * quads_fine, range(fine), 0, fine_rows, 0, 0)
        normalise(spec_coarse, z, 2 * quads_coarse, range(coarse), NYQ, 0, fine, 2 * quads_fine * fine)

    def cross(spec_ref, d, tile):
        a, b = spec_ref[0, tile], spec_ref[d, tile]
        ar, ai, br, bi = a[:, :LANES], a[:, LANES:], b[:, :LANES], b[:, LANES:]
        return [ar * br + ai * bi, ar * bi - ai * br]

    def tile_index(d, level, b, quad):
        index = (b * 2 + d) * quads_fine + quad
        if level:
            index = 2 * fine * quads_fine + (b * 2 + d) * quads_coarse + quad
        return index

    for level, (spec_ref, quads, blocks, first, nyquist, first_block) in enumerate((
        (spec_fine, quads_fine, fine, 0, fine_rows, 0),
        (spec_coarse, quads_coarse, coarse, NYQ, 0, fine),
    )):
        columns = [[] for _ in range(blocks)]
        for d in range(2):
            for quad in range(quads):
                value = jnp.concatenate(
                    cross(spec_ref, d + 1, 2 * quad) + cross(spec_ref, d + 1, 2 * quad + 1), axis=1)
                y = dot3(value, shift_ref)
                for b in range(blocks):
                    at = first + b * HALF
                    stack = jnp.concatenate(
                        [y[at : at + HALF, :LANES], y[at : at + HALF, LANES:],
                         y[nyquist : nyquist + NYQ, :LANES]], axis=0)
                    high, low = split(stack)
                    columns[b].append(jnp.concatenate([high, low], axis=0))
        for b in range(blocks):
            both = dot(map_ref[first_block + b], jnp.concatenate(columns[b], axis=1))
            maps = both[:WINDOW] + both[WINDOW:]
            for d in range(2):
                for quad in range(quads):
                    at = (d * quads + quad) * LANES
                    maps_ref[tile_index(d, level, b, quad)] = maps[:, at : at + LANES]

    lanes = lax.broadcasted_iota(jnp.int32, (maps_ref.shape[0], LANES), 1) // WINDOW
    for big in range(WINDOW // 4):
        rows = [maps_ref[:, 4 * big + r, :] for r in range(4)]
        for g in range(4):
            value = None
            for r in range(4):
                moved = rows[r] if r == g else pltpu.roll(rows[r], (WINDOW * (r - g)) % LANES, 1)
                value = moved if value is None else jnp.where(lanes == r, moved, value)
            at = big * LANES
            for level, (out, quads, blocks) in enumerate((
                (out_fine, quads_fine, fine), (out_coarse, quads_coarse, coarse))):
                for d in range(2):
                    for b in range(blocks):
                        start = tile_index(d, level, b, 0)
                        for quad in range(quads):
                            row = 4 * quad + g
                            out[0, d, b, row : row + 1, at : at + LANES] = value[start + quad : start + quad + 1]


def correlate(own, rim, near, rim_near, far, rim_far, masks, fine, coarse):
    strip_rows, width = own.shape
    quads_fine = width // STRIDE // 4
    quads_coarse = width // (2 * STRIDE) // 4
    tables = (row_table(strip_rows), fine_table(), coarse_table(), shift_table(), map_table(fine + coarse))
    half_rows = (fine + coarse) * HALF + NYQ
    whole = pl.BlockSpec(memory_space=pltpu.VMEM)
    return pl.pallas_call(
        functools.partial(kernel, fine, coarse, quads_fine, quads_coarse),
        out_shape=(
            jax.ShapeDtypeStruct((1, 2, fine, 4 * quads_fine, WINDOW * WINDOW), f32),
            jax.ShapeDtypeStruct((1, 2, coarse, 4 * quads_coarse, WINDOW * WINDOW), f32),
        ),
        in_specs=[whole] * (7 + len(tables)),
        out_specs=(whole, whole),
        scratch_shapes=[
            pltpu.VMEM((3, 2 * half_rows, width + LANES), f32),
            pltpu.VMEM((3, 2 * quads_fine, fine * HALF + NYQ, 2 * LANES), f32),
            pltpu.VMEM((3, 2 * quads_coarse, coarse * HALF + NYQ, 2 * LANES), f32),
            pltpu.VMEM((2 * (fine * quads_fine + coarse * quads_coarse), WINDOW, LANES), f32),
        ],
        compiler_params=pltpu.CompilerParams(vmem_limit_bytes=32 * 1024 * 1024),
    )(own, rim, near, rim_near, far, rim_far, masks, *(jnp.asarray(table) for table in tables))


def mask_rows(mask):
    blocks, patches = mask.shape
    quads = patches // 4
    tiles = mask.astype(f32).reshape(blocks, quads, 2, 2).transpose(1, 3, 0, 2)
    return jnp.repeat(tiles.reshape(2 * quads * blocks, 2), PATCH, axis=1)


def local(sections, mask_fine, mask_coarse):
    rim = shifted(sections, "strip", -1)
    near = shifted(sections, "sec", -1)
    far = shifted(sections, "sec", -2)
    rim_near = shifted(near, "strip", -1)
    rim_far = shifted(far, "strip", -1)
    masks = jnp.concatenate([mask_rows(mask_fine[0]), mask_rows(mask_coarse[0])], axis=0)
    return correlate(
        sections[0], rim[0], near[0], rim_near[0], far[0], rim_far[0], masks,
        mask_fine.shape[1], mask_coarse.shape[1])


def solution(mesh):
    in_specs = (
        P("sec", "strip", "groups"),
        P("sec", "strip", "groups"),
        P("sec", "strip", "groups"),
    )
    out_specs = (P("sec", None, "strip", "groups", None), P("sec", None, "strip", "groups", None))
    return jax.shard_map(local, mesh=mesh, in_specs=in_specs, out_specs=out_specs, check_vma=False)
```

profile of v0, /device:TPU:1, one launch (start us, length us, event | category | flops | bytes accessed | tf_op | source)
XLA Modules:
  0.0 31.9 jit_solution(11620826561263716614)
XLA Ops:
  0.6 2.1 %collective-permute-start = (bf16[1,64,512]{2,1,0:T(8,128)(2,1)}, bf16[1,64,512]{2,1,0:T(8,128)(2,1)S(1)}, u32[]{:S(2)}, u32[]{:S(2)}) collective-permute-start(bf16[1,64,512]{2,1,0:T(8,128)(2,1)} %param.8), channel_id=1, source_target_pairs={{1,0},{2,1},{3,2},{5,4},{6,5},{7,6},{9,8},{10,9},{11,10},{13,12},{... | collective-permute-start | bytes 196616 | tf_op jit(solution)/shard_map/ppermute | solution.py:25
  2.7 1.3 %collective-permute-start.3 = (bf16[1,64,512]{2,1,0:T(8,128)(2,1)}, bf16[1,64,512]{2,1,0:T(8,128)(2,1)S(1)}, u32[]{:S(2)}, u32[]{:S(2)}) collective-permute-start(bf16[1,64,512]{2,1,0:T(8,128)(2,1)} %param.8), channel_id=1, source_target_pairs={{8,0},{12,4},{9,1},{13,5},{10,2},{14,6},{11,3},{15,7},{24,16},{28,... | collective-permute-start | bytes 196616 | tf_op jit(solution)/shard_map/ppermute | solution.py:25
  4.0 1.3 %collective-permute-start.1 = (bf16[1,64,512]{2,1,0:T(8,128)(2,1)}, bf16[1,64,512]{2,1,0:T(8,128)(2,1)S(1)}, u32[]{:S(2)}, u32[]{:S(2)}) collective-permute-start(bf16[1,64,512]{2,1,0:T(8,128)(2,1)} %param.8), channel_id=1, source_target_pairs={{4,0},{8,4},{12,8},{5,1},{9,5},{13,9},{6,2},{10,6},{14,10},{7,3},{... | collective-permute-start | bytes 196616 | tf_op jit(solution)/shard_map/ppermute | solution.py:25
  5.3 0.7 %convert_element_type.22 = f32[1,2,16]{2,1,0:T(2,128)S(1)} convert(s32[1,2,16]{2,1,0:T(2,128)} %param.9) | non-fusion elementwise | flops 32 | bytes 256 | tf_op jit(solution)/shard_map/convert_element_type | solution.py:314
  6.0 0.7 %convert_reduce_fusion = f32[8]{0:T(128)S(1)} fusion(s32[1,1,8]{2,1,0:T(1,128)} %param.10), kind=kLoop, calls=%fused_computation.1 | loop fusion | flops 8 | bytes 64 | tf_op jit(solution)/shard_map/convert_element_type | solution.py:314
  6.7 0.1 convert_element_type.25
  6.8 0.1 copy.19
  6.9 0.1 broadcast_in_dim.7
  7.0 0.1 reshape.37
  7.1 0.1 convert_element_type.23
  7.1 0.1 copy.18
  7.3 0.1 broadcast_in_dim.6
  7.4 0.1 reshape.35
  7.4 2.5 %collective-permute-done.3 = bf16[1,64,512]{2,1,0:T(8,128)(2,1)S(1)} collective-permute-done((bf16[1,64,512]{2,1,0:T(8,128)(2,1)}, bf16[1,64,512]{2,1,0:T(8,128)(2,1)S(1)}, u32[]{:S(2)}, u32[]{:S(2)}) %collective-permute-start.3) | collective-permute-done | bytes 65568 | tf_op jit(solution)/shard_map/ppermute | solution.py:25
  10.0 2.2 %collective-permute-start.4 = (bf16[1,64,512]{2,1,0:T(8,128)(2,1)S(1)}, bf16[1,64,512]{2,1,0:T(8,128)(2,1)S(1)}, u32[]{:S(2)}, u32[]{:S(2)}) collective-permute-start(bf16[1,64,512]{2,1,0:T(8,128)(2,1)S(1)} %collective-permute-done.3), channel_id=1, source_target_pairs={{1,0},{2,1},{3,2},{5,4},{6,5},{7,6},{9,8},{10,9},{11,10},{13,12},{... | collective-permute-start | bytes 196616 | tf_op jit(solution)/shard_map/ppermute | solution.py:25
  12.2 1.9 %collective-permute-start.2 = (bf16[1,64,512]{2,1,0:T(8,128)(2,1)S(1)}, bf16[1,64,512]{2,1,0:T(8,128)(2,1)S(1)}, u32[]{:S(2)}, u32[]{:S(2)}) collective-permute-start(bf16[1,64,512]{2,1,0:T(8,128)(2,1)S(1)} %collective-permute-done.1), channel_id=1, source_target_pairs={{1,0},{2,1},{3,2},{5,4},{6,5},{7,6},{9,8},{10,9},{11,10},{13,12},{... | collective-permute-start | bytes 196616 | tf_op jit(solution)/shard_map/ppermute | solution.py:25
  14.1 4.2 %collective-permute-done.4 = bf16[1,64,512]{2,1,0:T(8,128)(2,1)S(1)} collective-permute-done((bf16[1,64,512]{2,1,0:T(8,128)(2,1)S(1)}, bf16[1,64,512]{2,1,0:T(8,128)(2,1)S(1)}, u32[]{:S(2)}, u32[]{:S(2)}) %collective-permute-start.4) | collective-permute-done | bytes 65568 | tf_op jit(solution)/shard_map/ppermute | solution.py:25
  18.3 1.9 %collective-permute-done.2 = bf16[1,64,512]{2,1,0:T(8,128)(2,1)S(1)} collective-permute-done((bf16[1,64,512]{2,1,0:T(8,128)(2,1)S(1)}, bf16[1,64,512]{2,1,0:T(8,128)(2,1)S(1)}, u32[]{:S(2)}, u32[]{:S(2)}) %collective-permute-start.2) | collective-permute-done | bytes 65568 | tf_op jit(solution)/shard_map/ppermute | solution.py:25
  20.2 1.1 %copy-done = bf16[1536,256]{1,0:T(8,128)(2,1)S(1)} copy-done((bf16[1536,256]{1,0:T(8,128)(2,1)S(1)}, bf16[1536,256]{1,0:T(8,128)(2,1)}, u32[]{:S(2)}) %copy-start) | copy-done | bytes 786456
  21.4 1.1 %copy-done.1 = bf16[1536,256]{1,0:T(8,128)(2,1)S(1)} copy-done((bf16[1536,256]{1,0:T(8,128)(2,1)S(1)}, bf16[1536,256]{1,0:T(8,128)(2,1)}, u32[]{:S(2)}) %copy-start.1) | copy-done | bytes 786456
  22.5 1.0 %copy-done.2 = bf16[768,256]{1,0:T(8,128)(2,1)S(1)} copy-done((bf16[768,256]{1,0:T(8,128)(2,1)S(1)}, bf16[768,256]{1,0:T(8,128)(2,1)}, u32[]{:S(2)}) %copy-start.2) | copy-done | bytes 393240
  23.5 0.9 %copy-done.4 = bf16[3,64,160]{2,1,0:T(8,128)(2,1)S(1)} copy-done((bf16[3,64,160]{2,1,0:T(8,128)(2,1)S(1)}, bf16[3,64,160]{2,1,0:T(8,128)(2,1)}, u32[]{:S(2)}) %copy-start.4) | copy-done | bytes 61464
  24.4 0.8 %copy-done.5 = bf16[1,64,512]{2,1,0:T(8,128)(2,1)S(1)} copy-done((bf16[1,64,512]{2,1,0:T(8,128)(2,1)S(1)}, bf16[1,64,512]{2,1,0:T(8,128)(2,1)}, u32[]{:S(2)}) %copy-start.5) | copy-done | bytes 65560
  25.2 6.6 %shard_map.95 = (f32[1,2,2,16,1024]{4,3,2,1,0:T(8,128)}, f32[1,2,1,8,1024]{4,3,2,1,0:T(8,128)}) custom-call(bf16[64,512]{1,0:T(8,128)(2,1)S(1)} %bitcast.10, bf16[64,512]{1,0:T(8,128)(2,1)S(1)} %bitcast.11, bf16[64,512]{1,0:T(8,128)(2,1)S(1)} %bitcast.13, bf16[64,512]{1,0:T(8,128)(2,1)S(1)} %bitcast.15, bf16[64,512]{1,0:T(8,128)(2,1)S(1)} %bitcast.12, ...), custom_call_target="tpu_custom_call" | custom-call | tf_op jit(solution)/shard_map/pallas_call | solution.py:293
  (10 shorter events, 0.0 us)
Async XLA Ops:
  0.6 19.6 %copy-start.3 = (bf16[224,256]{1,0:T(8,128)(2,1)S(1)}, bf16[224,256]{1,0:T(8,128)(2,1)}, u32[]{:S(2)}) copy-start(bf16[224,256]{1,0:T(8,128)(2,1)} %constant.10.clone.row_ref) | copy-start | bytes 344068
  0.6 13.5 %collective-permute-start = (bf16[1,64,512]{2,1,0:T(8,128)(2,1)}, bf16[1,64,512]{2,1,0:T(8,128)(2,1)S(1)}, u32[]{:S(2)}, u32[]{:S(2)}) collective-permute-start(bf16[1,64,512]{2,1,0:T(8,128)(2,1)} %param.8), channel_id=1, source_target_pairs={{1,0},{2,1},{3,2},{5,4},{6,5},{7,6},{9,8},{10,9},{11,10},{13,12},{... | collective-permute-start | bytes 196616 | tf_op jit(solution)/shard_map/ppermute | solution.py:25
  2.7 7.2 %collective-permute-start.3 = (bf16[1,64,512]{2,1,0:T(8,128)(2,1)}, bf16[1,64,512]{2,1,0:T(8,128)(2,1)S(1)}, u32[]{:S(2)}, u32[]{:S(2)}) collective-permute-start(bf16[1,64,512]{2,1,0:T(8,128)(2,1)} %param.8), channel_id=1, source_target_pairs={{8,0},{12,4},{9,1},{13,5},{10,2},{14,6},{11,3},{15,7},{24,16},{28,... | collective-permute-start | bytes 196616 | tf_op jit(solution)/shard_map/ppermute | solution.py:25
  4.0 8.1 %collective-permute-start.1 = (bf16[1,64,512]{2,1,0:T(8,128)(2,1)}, bf16[1,64,512]{2,1,0:T(8,128)(2,1)S(1)}, u32[]{:S(2)}, u32[]{:S(2)}) collective-permute-start(bf16[1,64,512]{2,1,0:T(8,128)(2,1)} %param.8), channel_id=1, source_target_pairs={{4,0},{8,4},{12,8},{5,1},{9,5},{13,9},{6,2},{10,6},{14,10},{7,3},{... | collective-permute-start | bytes 196616 | tf_op jit(solution)/shard_map/ppermute | solution.py:25
  10.0 8.3 %collective-permute-start.4 = (bf16[1,64,512]{2,1,0:T(8,128)(2,1)S(1)}, bf16[1,64,512]{2,1,0:T(8,128)(2,1)S(1)}, u32[]{:S(2)}, u32[]{:S(2)}) collective-permute-start(bf16[1,64,512]{2,1,0:T(8,128)(2,1)S(1)} %collective-permute-done.3), channel_id=1, source_target_pairs={{1,0},{2,1},{3,2},{5,4},{6,5},{7,6},{9,8},{10,9},{11,10},{13,12},{... | collective-permute-start | bytes 196616 | tf_op jit(solution)/shard_map/ppermute | solution.py:25
  12.2 8.0 %collective-permute-start.2 = (bf16[1,64,512]{2,1,0:T(8,128)(2,1)S(1)}, bf16[1,64,512]{2,1,0:T(8,128)(2,1)S(1)}, u32[]{:S(2)}, u32[]{:S(2)}) collective-permute-start(bf16[1,64,512]{2,1,0:T(8,128)(2,1)S(1)} %collective-permute-done.1), channel_id=1, source_target_pairs={{1,0},{2,1},{3,2},{5,4},{6,5},{7,6},{9,8},{10,9},{11,10},{13,12},{... | collective-permute-start | bytes 196616 | tf_op jit(solution)/shard_map/ppermute | solution.py:25
  20.2 1.1 %copy-start = (bf16[1536,256]{1,0:T(8,128)(2,1)S(1)}, bf16[1536,256]{1,0:T(8,128)(2,1)}, u32[]{:S(2)}) copy-start(bf16[1536,256]{1,0:T(8,128)(2,1)} %constant.13.clone.shift_ref) | copy-start | bytes 2359300
  21.4 1.1 %copy-start.1 = (bf16[1536,256]{1,0:T(8,128)(2,1)S(1)}, bf16[1536,256]{1,0:T(8,128)(2,1)}, u32[]{:S(2)}) copy-start(bf16[1536,256]{1,0:T(8,128)(2,1)} %constant.12.clone.coarse_ref) | copy-start | bytes 2359300
  22.5 1.0 %copy-start.2 = (bf16[768,256]{1,0:T(8,128)(2,1)S(1)}, bf16[768,256]{1,0:T(8,128)(2,1)}, u32[]{:S(2)}) copy-start(bf16[768,256]{1,0:T(8,128)(2,1)} %constant.11.clone.fine_ref) | copy-start | bytes 1179652
  23.5 0.9 %copy-start.4 = (bf16[3,64,160]{2,1,0:T(8,128)(2,1)S(1)}, bf16[3,64,160]{2,1,0:T(8,128)(2,1)}, u32[]{:S(2)}) copy-start(bf16[3,64,160]{2,1,0:T(8,128)(2,1)} %constant.14.clone.map_ref) | copy-start | bytes 184324
  24.4 0.8 %copy-start.5 = (bf16[1,64,512]{2,1,0:T(8,128)(2,1)S(1)}, bf16[1,64,512]{2,1,0:T(8,128)(2,1)}, u32[]{:S(2)}) copy-start(bf16[1,64,512]{2,1,0:T(8,128)(2,1)} %param.8) | copy-start | bytes 196612
where the time goes:
time: 32.3 us; the launch traced here: 31.9 us
  starting transfers between devices  8.8 us (27%)
  waiting for transfers between devices  8.62 us (27%)
  Pallas kernels  6.63 us (21%)
  local copies, waits for them, and re-layouts  5.73 us (18%)
  other arithmetic  1.36 us (4%)
  between operations  0.72 us (2%)
    ppermute x5, starting transfers between devices, shifted(): lax.ppermute(value, axis, [(source, source + steps) for source in range(l...  8.8 us
    ppermute x5, waiting for transfers between devices, shifted(): lax.ppermute(value, axis, [(source, source + steps) for source in range(l...  8.62 us
    pallas_call x1, Pallas kernels, correlate(): pl.pallas_call(functools.partial(kernel, fine, coarse, quads_fine, quads_...  6.63 us
    unnamed x12, local copies, waits for them, and re-layouts  5 us
    convert_element_type x2, other arithmetic, mask_rows(): tiles = mask.astype(f32).reshape(blocks, quads, 2, 2).transpose(1, 3, 0, 2)  1.35 us
  transfers between devices with their start and end apart: 5, of which 3 were waited for; matrix products, arithmetic and copies ran while one was open for 7% of the time, Pallas kernels for 0%

commit v1 on v0

--- a/solution.py
+++ b/solution.py
@@ -65,8 +65,7 @@
 
 
 def stacked(table):
-    high, low = split_table(table)
-    return np.concatenate([high, high, low], axis=0)
+    return np.concatenate(split_table(table), axis=0)
 
 
 def fine_table():
@@ -115,8 +114,16 @@
         high, low = split_table(np.concatenate([c * weight, -s * weight, nyquist], axis=1))
         top = np.concatenate([high, high], axis=1)
         bottom = np.concatenate([low, np.zeros_like(low)], axis=1)
-        rows.append(np.concatenate([top, bottom], axis=0))
-    return np.stack(rows)
+        rows += [top, bottom]
+    return np.concatenate(rows)
+
+
+def all_tables(strip_rows, blocks):
+    tables = [row_table(strip_rows), fine_table(), coarse_table(), shift_table(), map_table(blocks)]
+    width = max(table.shape[1] for table in tables)
+    places = np.cumsum([0] + [table.shape[0] for table in tables])[:-1]
+    padded = [np.pad(table, ((0, 0), (0, width - table.shape[1]))) for table in tables]
+    return np.concatenate(padded), tuple(int(place) for place in places)
 
 
 def split(value):
@@ -128,19 +135,24 @@
     return jnp.dot(left, right, preferred_element_type=f32)
 
 
-def dot3(value, table_ref):
+def dot3(value, table_ref, at):
     high, low = split(value)
-    return dot(jnp.concatenate([high, low, high], axis=1), table_ref[...])
+    depth = value.shape[1]
+    table_high = table_ref[at : at + depth]
+    table_low = table_ref[at + depth : at + 2 * depth]
+    return dot(
+        jnp.concatenate([high, low, high], axis=1),
+        jnp.concatenate([table_high, table_high, table_low], axis=0))
 
 
 def kernel(
-    fine, coarse, quads_fine, quads_coarse,
-    own, rim, near, rim_near, far, rim_far, mask_ref,
-    row_ref, fine_ref, coarse_ref, shift_ref, map_ref,
+    fine, coarse, quads_fine, quads_coarse, places,
+    strips, rims, mask_fine, mask_coarse, table_ref,
     out_fine, out_coarse,
-    t_ref, spec_fine, spec_coarse, maps_ref,
+    t_ref, spec_fine, spec_coarse, maps_ref, rows_ref,
 ):
-    width = own.shape[1]
+    width = strips.shape[2]
+    row_at, fine_at, coarse_at, shift_at, map_at = places
     fine_rows = fine * HALF
     fine_all = fine_rows + NYQ
     coarse_rows = coarse * HALF
@@ -153,9 +165,9 @@
     ones = jnp.where(same, 1.0, 0.0).astype(bf16)
     ones = jnp.concatenate([ones, ones], axis=0)
 
-    for z, (top, bottom) in enumerate(((own, rim), (near, rim_near), (far, rim_far))):
-        x = jnp.concatenate([top[...], bottom[...]], axis=0)
-        t = dot(row_ref[...], jnp.concatenate([x, x], axis=0))
+    for z in range(3):
+        x = jnp.concatenate([strips[z], rims[z]], axis=0)
+        t = dot(table_ref[row_at : row_at + 2 * half_rows], jnp.concatenate([x, x], axis=0))
         t_ref[z, :, :width] = t
         t_ref[z, :, width:] = jnp.zeros((2 * half_rows, LANES), f32)
 
@@ -172,7 +184,7 @@
         tail = q[nyquist_row[0] : nyquist_row[0] + 8]
         return 2.0 * total - head + jnp.where(sub == nyquist_row[1], tail, 0.0)
 
-    def normalise(spec_ref, z, tiles, blocks, block_first, nyquist_first, first_block, first_mask):
+    def normalise(spec_ref, z, tiles, blocks, block_first, nyquist_first, first_block, mask_ref):
         rows = len(blocks)
         sums = []
         for tile in range(tiles):
@@ -190,8 +202,9 @@
                 total = jnp.sum(stack[at : at + 8], axis=0, keepdims=True)
                 scale = 1.0 / jnp.sqrt(total * (1.0 / PATCH**4) + 1e-05)
                 if z == 0:
-                    m = first_mask + tile * rows + b
-                    scale = scale * mask_ref[m : m + 1, :]
+                    patch = 4 * (tile // 2) + tile % 2
+                    kept = jnp.where(lane[:1] < PATCH, mask_ref[0, b, patch], mask_ref[0, b, patch + 2])
+                    scale = scale * kept.astype(f32)
                 scales.append(jnp.concatenate([scale, scale], axis=1))
             parts = {}
             for b in range(rows):
@@ -216,7 +229,7 @@
                 value = jnp.concatenate(
                     [t_ref[z, :fine_all, at : at + LANES],
                      t_ref[z, half_rows : half_rows + fine_all, at : at + LANES]], axis=1)
-                spec_fine[z, 2 * m + odd] = dot3(value, fine_ref)
+                spec_fine[z, 2 * m + odd] = dot3(value, table_ref, fine_at)
         for n in range(quads_coarse):
             for odd in range(2):
                 pieces = []
@@ -224,9 +237,9 @@
                     at = 2 * LANES * n + LANES * p + 2 * STRIDE * odd
                     pieces += [t_ref[z, fine_rows:half_rows, at : at + LANES],
                                t_ref[z, half_rows + fine_rows : 2 * half_rows, at : at + LANES]]
-                spec_coarse[z, 2 * n + odd] = dot3(jnp.concatenate(pieces, axis=1), coarse_ref)
-        normalise(spec_fine, z, 2 * quads_fine, range(fine), 0, fine_rows, 0, 0)
-        normalise(spec_coarse, z, 2 * quads_coarse, range(coarse), NYQ, 0, fine, 2 * quads_fine * fine)
+                spec_coarse[z, 2 * n + odd] = dot3(jnp.concatenate(pieces, axis=1), table_ref, coarse_at)
+        normalise(spec_fine, z, 2 * quads_fine, range(fine), 0, fine_rows, 0, mask_fine)
+        normalise(spec_coarse, z, 2 * quads_coarse, range(coarse), NYQ, 0, fine, mask_coarse)
 
     def cross(spec_ref, d, tile):
         a, b = spec_ref[0, tile], spec_ref[d, tile]
@@ -248,7 +261,7 @@
             for quad in range(quads):
                 value = jnp.concatenate(
                     cross(spec_ref, d + 1, 2 * quad) + cross(spec_ref, d + 1, 2 * quad + 1), axis=1)
-                y = dot3(value, shift_ref)
+                y = dot3(value, table_ref, shift_at)
                 for b in range(blocks):
                     at = first + b * HALF
                     stack = jnp.concatenate(
@@ -257,7 +270,9 @@
                     high, low = split(stack)
                     columns[b].append(jnp.concatenate([high, low], axis=0))
         for b in range(blocks):
-            both = dot(map_ref[first_block + b], jnp.concatenate(columns[b], axis=1))
+            at = map_at + 2 * WINDOW * (first_block + b)
+            columns_b = jnp.concatenate(columns[b], axis=1)
+            both = dot(table_ref[at : at + 2 * WINDOW, : columns_b.shape[0]], columns_b)
             maps = both[:WINDOW] + both[WINDOW:]
             for d in range(2):
                 for quad in range(quads):
@@ -272,59 +287,49 @@
             for r in range(4):
                 moved = rows[r] if r == g else pltpu.roll(rows[r], (WINDOW * (r - g)) % LANES, 1)
                 value = moved if value is None else jnp.where(lanes == r, moved, value)
-            at = big * LANES
-            for level, (out, quads, blocks) in enumerate((
-                (out_fine, quads_fine, fine), (out_coarse, quads_coarse, coarse))):
-                for d in range(2):
-                    for b in range(blocks):
-                        start = tile_index(d, level, b, 0)
-                        for quad in range(quads):
-                            row = 4 * quad + g
-                            out[0, d, b, row : row + 1, at : at + LANES] = value[start + quad : start + quad + 1]
-
-
-def correlate(own, rim, near, rim_near, far, rim_far, masks, fine, coarse):
-    strip_rows, width = own.shape
+            rows_ref[big, pl.ds(g, maps_ref.shape[0], stride=4), :] = value
+        for out, level, quads, blocks in ((out_fine, 0, quads_fine, fine), (out_coarse, 1, quads_coarse, coarse)):
+            for d in range(2):
+                for b in range(blocks):
+                    at = 4 * tile_index(d, level, b, 0)
+                    out[0, d, b, :, big * LANES : (big + 1) * LANES] = rows_ref[big, at : at + 4 * quads]
+
+
+def correlate(strips, rims, mask_fine, mask_coarse):
+    strip_rows, width = strips.shape[1:]
+    fine, coarse = mask_fine.shape[1], mask_coarse.shape[1]
     quads_fine = width // STRIDE // 4
     quads_coarse = width // (2 * STRIDE) // 4
-    tables = (row_table(strip_rows), fine_table(), coarse_table(), shift_table(), map_table(fine + coarse))
+    table, places = all_tables(strip_rows, fine + coarse)
     half_rows = (fine + coarse) * HALF + NYQ
+    tiles = 2 * (fine * quads_fine + coarse * quads_coarse)
     whole = pl.BlockSpec(memory_space=pltpu.VMEM)
+    scalars = pl.BlockSpec(memory_space=pltpu.SMEM)
     return pl.pallas_call(
-        functools.partial(kernel, fine, coarse, quads_fine, quads_coarse),
+        functools.partial(kernel, fine, coarse, quads_fine, quads_coarse, places),
         out_shape=(
             jax.ShapeDtypeStruct((1, 2, fine, 4 * quads_fine, WINDOW * WINDOW), f32),
             jax.ShapeDtypeStruct((1, 2, coarse, 4 * quads_coarse, WINDOW * WINDOW), f32),
         ),
-        in_specs=[whole] * (7 + len(tables)),
+        in_specs=[whole, whole, scalars, scalars, whole],
         out_specs=(whole, whole),
         scratch_shapes=[
             pltpu.VMEM((3, 2 * half_rows, width + LANES), f32),
             pltpu.VMEM((3, 2 * quads_fine, fine * HALF + NYQ, 2 * LANES), f32),
             pltpu.VMEM((3, 2 * quads_coarse, coarse * HALF + NYQ, 2 * LANES), f32),
-            pltpu.VMEM((2 * (fine * quads_fine + coarse * quads_coarse), WINDOW, LANES), f32),
+            pltpu.VMEM((tiles, WINDOW, LANES), f32),
+            pltpu.VMEM((WINDOW // 4, 4 * tiles, LANES), f32),
         ],
         compiler_params=pltpu.CompilerParams(vmem_limit_bytes=32 * 1024 * 1024),
-    )(own, rim, near, rim_near, far, rim_far, masks, *(jnp.asarray(table) for table in tables))
-
-
-def mask_rows(mask):
-    blocks, patches = mask.shape
-    quads = patches // 4
-    tiles = mask.astype(f32).reshape(blocks, quads, 2, 2).transpose(1, 3, 0, 2)
-    return jnp.repeat(tiles.reshape(2 * quads * blocks, 2), PATCH, axis=1)
+    )(strips, rims, mask_fine, mask_coarse, jnp.asarray(table))
 
 
 def local(sections, mask_fine, mask_coarse):
-    rim = shifted(sections, "strip", -1)
     near = shifted(sections, "sec", -1)
     far = shifted(sections, "sec", -2)
-    rim_near = shifted(near, "strip", -1)
-    rim_far = shifted(far, "strip", -1)
-    masks = jnp.concatenate([mask_rows(mask_fine[0]), mask_rows(mask_coarse[0])], axis=0)
-    return correlate(
-        sections[0], rim[0], near[0], rim_near[0], far[0], rim_far[0], masks,
-        mask_fine.shape[1], mask_coarse.shape[1])
+    strips = jnp.concatenate([sections, near, far], axis=0)
+    rims = shifted(strips, "strip", -1)
+    return correlate(strips, rims, mask_fine, mask_coarse)
 
 
 def solution(mesh):

time: 32.3 us -> 28.3 us (0.88)
  starting transfers between devices: 8.8 us -> 6.2 us
  local copies, waits for them, and re-layouts: 5.73 us -> 3.58 us
  waiting for transfers between devices: 8.62 us -> 10.3 us
  other arithmetic: 1.36 us -> 0 us
  Pallas kernels: 6.63 us -> 7.29 us
    ppermute x5 -> x3, starting transfers between devices: 8.8 us -> 6.2 us  [shifted(): lax.ppermute(value, axis, [(source, source + steps) for source in range(l...]
    ppermute x5 -> x3, waiting for transfers between devices: 8.62 us -> 10.3 us  [shifted(): lax.ppermute(value, axis, [(source, source + steps) for source in range(l...]
    unnamed x12 -> x8, local copies, waits for them, and re-layouts: 5 us -> 3.57 us
    convert_element_type x2 -> x0, other arithmetic: 1.35 us -> none  [mask_rows(): tiles = mask.astype(f32).reshape(blocks, quads, 2, 2).transpose(1, 3, 0, 2)]
    pallas_call x1, Pallas kernels: 6.63 us -> 7.29 us  [correlate(): pl.pallas_call(functools.partial(kernel, fine, coarse, quads_fine, quads_...]
    reshape x4 -> x0, local copies, waits for them, and re-layouts: 0.41 us -> none  [mask_rows(): return jnp.repeat(tiles.reshape(2 * quads * blocks, 2), PATCH, axis=1)]
  transfers between devices with their start and end apart: 5 -> 3, of which waited for: 3 -> 3; matrix products, arithmetic and copies ran while one was open for 7% -> 3% of each run, Pallas kernels for 0% -> 0%
where the time goes in v1:
time: 28.3 us; the launch traced here: 28 us
  waiting for transfers between devices  10.3 us (36%)
  Pallas kernels  7.29 us (26%)
  starting transfers between devices  6.2 us (22%)
  local copies, waits for them, and re-layouts  3.58 us (13%)
  between operations  0.66 us (2%)
    ppermute x3, waiting for transfers between devices, shifted(): lax.ppermute(value, axis, [(source, source + steps) for source in range(l...  10.3 us
    pallas_call x1, Pallas kernels, correlate(): pl.pallas_call(functools.partial(kernel, fine, coarse, quads_fine, quads_...  7.29 us
    ppermute x3, starting transfers between devices, shifted(): lax.ppermute(value, axis, [(source, source + steps) for source in range(l...  6.2 us
    unnamed x8, local copies, waits for them, and re-layouts  3.57 us
  transfers between devices with their start and end apart: 3, of which 3 were waited for; matrix products, arithmetic and copies ran while one was open for 3% of the time, Pallas kernels for 0%

profile of v1, /device:TPU:1, one launch (start us, length us, event | category | flops | bytes accessed | tf_op | source)
XLA Modules:
  0.0 28.0 jit_solution(15873135142645090995)
XLA Ops:
  0.6 1.3 %collective-permute-start = (bf16[1,64,512]{2,1,0:T(8,128)(2,1)}, bf16[1,64,512]{2,1,0:T(8,128)(2,1)S(1)}, u32[]{:S(2)}, u32[]{:S(2)}) collective-permute-start(bf16[1,64,512]{2,1,0:T(8,128)(2,1)} %param.4), channel_id=1, source_target_pairs={{4,0},{8,4},{12,8},{5,1},{9,5},{13,9},{6,2},{10,6},{14,10},{7,3},{... | collective-permute-start | bytes 196616 | tf_op jit(solution)/shard_map/ppermute | solution.py:25
  1.9 1.3 %collective-permute-start.1 = (bf16[1,64,512]{2,1,0:T(8,128)(2,1)}, bf16[1,64,512]{2,1,0:T(8,128)(2,1)S(1)}, u32[]{:S(2)}, u32[]{:S(2)}) collective-permute-start(bf16[1,64,512]{2,1,0:T(8,128)(2,1)} %param.4), channel_id=1, source_target_pairs={{8,0},{12,4},{9,1},{13,5},{10,2},{14,6},{11,3},{15,7},{24,16},{28,... | collective-permute-start | bytes 196616 | tf_op jit(solution)/shard_map/ppermute | solution.py:25
  3.2 0.8 %constant_dynamic-update-slice_fusion.2 = bf16[3,64,512]{2,1,0:T(8,128)(2,1)S(1)} fusion(bf16[1,64,512]{2,1,0:T(8,128)(2,1)} %param.4), kind=kLoop, calls=%fused_computation.2 | loop fusion | bytes 131072
  4.1 2.4 %collective-permute-done = bf16[1,64,512]{2,1,0:T(8,128)(2,1)S(1)} collective-permute-done((bf16[1,64,512]{2,1,0:T(8,128)(2,1)}, bf16[1,64,512]{2,1,0:T(8,128)(2,1)S(1)}, u32[]{:S(2)}, u32[]{:S(2)}) %collective-permute-start) | collective-permute-done | bytes 65568 | tf_op jit(solution)/shard_map/ppermute | solution.py:25
  6.5 3.4 %collective-permute-done.1 = bf16[1,64,512]{2,1,0:T(8,128)(2,1)S(1)} collective-permute-done((bf16[1,64,512]{2,1,0:T(8,128)(2,1)}, bf16[1,64,512]{2,1,0:T(8,128)(2,1)S(1)}, u32[]{:S(2)}, u32[]{:S(2)}) %collective-permute-start.1) | collective-permute-done | bytes 65568 | tf_op jit(solution)/shard_map/ppermute | solution.py:25
  9.9 3.6 %collective-permute-start.2 = (bf16[3,64,512]{2,1,0:T(8,128)(2,1)S(1)}, bf16[3,64,512]{2,1,0:T(8,128)(2,1)S(1)}, u32[]{:S(2)}, u32[]{:S(2)}) collective-permute-start(bf16[3,64,512]{2,1,0:T(8,128)(2,1)S(1)} %constant_dynamic-update-slice_fusion.strips), channel_id=1, source_target_pairs={{1,0},{2,1},{3,2},{5,4},{6,5},{7,6},{9,8},{10,9},{11,10},{13,12},{... | collective-permute-start | bytes 589832 | tf_op jit(solution)/shard_map/ppermute | solution.py:25
  13.5 4.4 %collective-permute-done.2.rims = bf16[3,64,512]{2,1,0:T(8,128)(2,1)S(1)} collective-permute-done((bf16[3,64,512]{2,1,0:T(8,128)(2,1)S(1)}, bf16[3,64,512]{2,1,0:T(8,128)(2,1)S(1)}, u32[]{:S(2)}, u32[]{:S(2)}) %collective-permute-start.2) | collective-permute-done | bytes 196640 | tf_op jit(solution)/shard_map/ppermute | solution.py:25
  18.0 0.0 copy-start
  18.0 1.4 %copy-done = bf16[2976,256]{1,0:T(8,128)(2,1)S(1)} copy-done((bf16[2976,256]{1,0:T(8,128)(2,1)S(1)}, bf16[2976,256]{1,0:T(8,128)(2,1)}, u32[]{:S(2)}) %copy-start) | copy-done | bytes 1523736
  19.4 0.0 copy-start.1
  19.4 0.7 %copy-done.1 = s32[1,2,16]{2,1,0:T(2,128)S(1)} copy-done((s32[1,2,16]{2,1,0:T(2,128)S(1)}, s32[1,2,16]{2,1,0:T(2,128)}, u32[]{:S(2)}) %copy-start.1) | copy-done | bytes 152
  20.0 0.0 copy-start.2
  20.0 0.7 %copy-done.2 = s32[1,1,8]{2,1,0:T(1,128)S(1)} copy-done((s32[1,1,8]{2,1,0:T(1,128)S(1)}, s32[1,1,8]{2,1,0:T(1,128)}, u32[]{:S(2)}) %copy-start.2) | copy-done | bytes 56
  20.7 7.3 %shard_map.59 = (f32[1,2,2,16,1024]{4,3,2,1,0:T(8,128)}, f32[1,2,1,8,1024]{4,3,2,1,0:T(8,128)}) custom-call(bf16[3,64,512]{2,1,0:T(8,128)(2,1)S(1)} %constant_dynamic-update-slice_fusion.strips, bf16[3,64,512]{2,1,0:T(8,128)(2,1)S(1)} %collective-permute-done.2.rims, s32[1,2,16]{2,1,0:T(2,128)S(1)} %copy-done.1, s32[1,1,8]{2,1,0:T(1,128)S(1)} %copy-done.2, ...), custom_call_target="tpu_custom_call" | custom-call | tf_op jit(solution)/shard_map/pallas_call | solution.py:308
  (2 shorter events, 0.0 us)
Async XLA Ops:
  0.6 5.9 %collective-permute-start = (bf16[1,64,512]{2,1,0:T(8,128)(2,1)}, bf16[1,64,512]{2,1,0:T(8,128)(2,1)S(1)}, u32[]{:S(2)}, u32[]{:S(2)}) collective-permute-start(bf16[1,64,512]{2,1,0:T(8,128)(2,1)} %param.4), channel_id=1, source_target_pairs={{4,0},{8,4},{12,8},{5,1},{9,5},{13,9},{6,2},{10,6},{14,10},{7,3},{... | collective-permute-start | bytes 196616 | tf_op jit(solution)/shard_map/ppermute | solution.py:25
  1.9 8.0 %collective-permute-start.1 = (bf16[1,64,512]{2,1,0:T(8,128)(2,1)}, bf16[1,64,512]{2,1,0:T(8,128)(2,1)S(1)}, u32[]{:S(2)}, u32[]{:S(2)}) collective-permute-start(bf16[1,64,512]{2,1,0:T(8,128)(2,1)} %param.4), channel_id=1, source_target_pairs={{8,0},{12,4},{9,1},{13,5},{10,2},{14,6},{11,3},{15,7},{24,16},{28,... | collective-permute-start | bytes 196616 | tf_op jit(solution)/shard_map/ppermute | solution.py:25
  9.9 8.1 %collective-permute-start.2 = (bf16[3,64,512]{2,1,0:T(8,128)(2,1)S(1)}, bf16[3,64,512]{2,1,0:T(8,128)(2,1)S(1)}, u32[]{:S(2)}, u32[]{:S(2)}) collective-permute-start(bf16[3,64,512]{2,1,0:T(8,128)(2,1)S(1)} %constant_dynamic-update-slice_fusion.strips), channel_id=1, source_target_pairs={{1,0},{2,1},{3,2},{5,4},{6,5},{7,6},{9,8},{10,9},{11,10},{13,12},{... | collective-permute-start | bytes 589832 | tf_op jit(solution)/shard_map/ppermute | solution.py:25
  18.0 1.4 %copy-start = (bf16[2976,256]{1,0:T(8,128)(2,1)S(1)}, bf16[2976,256]{1,0:T(8,128)(2,1)}, u32[]{:S(2)}) copy-start(bf16[2976,256]{1,0:T(8,128)(2,1)} %constant.2.clone.table_ref) | copy-start | bytes 4571140
  19.4 0.7 %copy-start.1 = (s32[1,2,16]{2,1,0:T(2,128)S(1)}, s32[1,2,16]{2,1,0:T(2,128)}, u32[]{:S(2)}) copy-start(s32[1,2,16]{2,1,0:T(2,128)} %mask_fine.1) | copy-start | bytes 388
  20.0 0.7 %copy-start.2 = (s32[1,1,8]{2,1,0:T(1,128)S(1)}, s32[1,1,8]{2,1,0:T(1,128)}, u32[]{:S(2)}) copy-start(s32[1,1,8]{2,1,0:T(1,128)} %mask_coarse.1) | copy-start | bytes 100

commit v2 on v1

v2 whole, which is shorter than its diff:
```python
import functools

import jax
import jax.numpy as jnp
import numpy as np
from jax import lax
from jax.experimental import pallas as pl
from jax.experimental.pallas import tpu as pltpu
from jax.sharding import PartitionSpec as P

PATCH = 64
STRIDE = 32
WINDOW = 32
HALF = PATCH // 2
LANES = 128
NYQ = 16

f32 = jnp.float32
bf16 = jnp.bfloat16


def from_device(value, sec_steps, strip_steps):
    secs, strips = lax.axis_size("sec"), lax.axis_size("strip")
    pairs = []
    for sec in range(secs - sec_steps):
        for strip in range(strips - strip_steps):
            pairs.append(((sec + sec_steps) * strips + strip + strip_steps, sec * strips + strip))
    return lax.ppermute(value, ("sec", "strip"), pairs)


def wave(phase):
    turns = np.arange(PATCH) * (2 * np.pi / PATCH)
    cos = np.round(np.cos(turns), 14)
    sin = np.round(np.sin(turns), 14)
    phase = np.mod(phase, PATCH)
    return cos[phase], sin[phase]


def split_table(table):
    high = table.astype(jnp.bfloat16)
    low = (table - high.astype(np.float64)).astype(jnp.bfloat16)
    return high, low


def row_table(ext, fine, coarse):
    k = np.arange(HALF)[:, None]
    cos_rows, sin_rows, nyquist = [], [], np.zeros((NYQ, ext))
    blocks = [(b * STRIDE, 1) for b in fine] + [(b * 2 * STRIDE, 2) for b in coarse]
    for at, (first, pool) in enumerate(blocks):
        cos = np.zeros((HALF, ext))
        sin = np.zeros((HALF, ext))
        x = np.arange(pool * PATCH) // pool
        c, s = wave(k * x[None, :])
        cos[:, first : first + x.size] = c / pool
        sin[:, first : first + x.size] = s / pool
        nyquist[at, first : first + x.size] = wave(HALF * x)[0] / pool
        cos_rows.append(cos)
        sin_rows.append(sin)
    n = len(fine)
    table = np.concatenate(
        cos_rows[:n] + [nyquist] + cos_rows[n:] + sin_rows[:n] + [np.zeros((NYQ, ext))] + sin_rows[n:])
    return np.concatenate(split_table(table), axis=1)


def stacked(table):
    return np.concatenate(split_table(table), axis=0)


def fine_table():
    c, s = wave(np.arange(PATCH)[:, None] * np.arange(PATCH)[None, :])
    table = np.zeros((2, 2, PATCH, 2, 2, PATCH))
    for p in range(2):
        table[0, p, :, 0, p] = c
        table[1, p, :, 0, p] = -s
        table[0, p, :, 1, p] = -s
        table[1, p, :, 1, p] = -c
    return stacked(table.reshape(4 * PATCH, 4 * PATCH))


def coarse_table():
    c, s = wave((np.arange(2 * PATCH) // 2)[:, None] * np.arange(PATCH)[None, :])
    table = np.zeros((2, 2, 2 * PATCH, 2, 2, PATCH))
    for p in range(2):
        table[p, 0, :, 0, p] = 0.5 * c
        table[p, 1, :, 0, p] = -0.5 * s
        table[p, 0, :, 1, p] = -0.5 * s
        table[p, 1, :, 1, p] = -0.5 * c
    return stacked(table.reshape(8 * PATCH, 4 * PATCH))


def shift_table():
    t = np.arange(WINDOW) - WINDOW // 2
    c, s = wave(np.arange(PATCH)[:, None] * t[None, :])
    table = np.zeros((2, 2, 2, PATCH, 2, 4, WINDOW))
    for odd in range(2):
        for p in range(2):
            table[odd, 0, p, :, 0, 2 * p + odd] = c
            table[odd, 1, p, :, 0, 2 * p + odd] = -s
            table[odd, 0, p, :, 1, 2 * p + odd] = s
            table[odd, 1, p, :, 1, 2 * p + odd] = c
    return stacked(table.reshape(8 * PATCH, 8 * WINDOW))


def map_table(blocks):
    shift = np.arange(WINDOW) - WINDOW // 2
    c, s = wave(shift[:, None] * np.arange(HALF)[None, :])
    weight = np.where(np.arange(HALF) == 0, 1.0, 2.0) / PATCH**3
    rows = []
    for block in range(blocks):
        nyquist = np.zeros((WINDOW, NYQ))
        nyquist[:, block] = wave(HALF * shift)[0] / PATCH**3
        high, low = split_table(np.concatenate([c * weight, -s * weight, nyquist], axis=1))
        rows += [np.concatenate([high, high], axis=1), np.concatenate([low, np.zeros_like(low)], axis=1)]
    return np.concatenate(rows)


def all_tables(ext, groups):
    tables = [row_table(ext, *group) for group in groups]
    tables += [fine_table(), shift_table(), map_table(max(len(f) + len(c) for f, c in groups)), coarse_table()]
    width = max(table.shape[1] for table in tables)
    places = np.cumsum([0] + [table.shape[0] for table in tables])
    padded = [np.pad(table, ((0, 0), (0, width - table.shape[1]))) for table in tables]
    return np.concatenate(padded), [int(place) for place in places]


def split(value):
    high = value.astype(bf16)
    return high, (value - high.astype(f32)).astype(bf16)


def dot(left, right):
    return jnp.dot(left, right, preferred_element_type=f32)


def dot3(high, low, table_ref, at):
    depth = high.shape[1]
    table_high = table_ref[at : at + depth]
    table_low = table_ref[at + depth : at + 2 * depth]
    return dot(
        jnp.concatenate([high, low, high], axis=1),
        jnp.concatenate([table_high, table_high, table_low], axis=0))


def power(values, first, nyquist, block, dc, sub):
    re, im = values[:, :LANES], values[:, LANES:]
    q = re * re + im * im
    total = None
    for r in range(0, HALF, 8):
        part = q[first + r : first + r + 8]
        if r == 0:
            part = jnp.where(dc, 0.0, part)
            head = jnp.where(sub == 0, part, 0.0)
        total = part if total is None else total + part
    return 2.0 * total - head + jnp.where(sub == block, q[nyquist : nyquist + 8], 0.0)


def normalise(spec_ref, z, tiles, rows, block_first, nyquist, first_block):
    sub = lax.broadcasted_iota(jnp.int32, (8, LANES), 0)
    lane = lax.broadcasted_iota(jnp.int32, (8, LANES), 1)
    dc = (sub == 0) & (lane % PATCH == 0)
    dc_both = jnp.concatenate([dc, dc], axis=1)
    group = lax.broadcasted_iota(jnp.int32, (LANES, LANES), 0) // PATCH
    same = group == lax.broadcasted_iota(jnp.int32, (LANES, LANES), 1) // PATCH
    ones = jnp.where(same, 1.0, 0.0).astype(bf16)
    sums = []
    for tile in range(tiles):
        values = spec_ref[z, tile]
        for b in range(rows):
            sums.append(power(values, block_first + b * HALF, nyquist, first_block + b, dc, sub))
    high, low = split(jnp.concatenate(sums, axis=0))
    stack = dot(jnp.concatenate([high, low], axis=1), jnp.concatenate([ones, ones], axis=0))
    nyquist_row = lax.broadcasted_iota(jnp.int32, (NYQ, 2 * LANES), 0)
    for tile in range(tiles):
        values = spec_ref[z, tile]
        parts = {}
        nyq = values[nyquist : nyquist + NYQ]
        scaled = jnp.zeros_like(nyq)
        for b in range(rows):
            at = (tile * rows + b) * 8
            total = jnp.sum(stack[at : at + 8], axis=0, keepdims=True)
            scale = 1.0 / jnp.sqrt(total * (1.0 / PATCH**4) + 1e-05)
            scale = jnp.concatenate([scale, scale], axis=1)
            first = block_first + b * HALF
            block = values[first : first + HALF]
            block = jnp.concatenate([jnp.where(dc_both, 0.0, block[:8]), block[8:]], axis=0)
            parts[first] = block * scale
            scaled = jnp.where(nyquist_row == first_block + b, nyq * scale, scaled)
        parts[nyquist] = scaled
        result = jnp.concatenate([parts[first] for first in sorted(parts)], axis=0)
        spec_ref[z, tile] = result.astype(bf16).astype(f32)


def maps_of(fine, coarse, width, strips, masks, table_ref, places, outs, scratch):
    row_at, fine_at, shift_at, map_at, coarse_at = places
    high_ref, low_ref, spec_fine, spec_coarse, maps_ref, rows_ref = scratch
    quads_fine, quads_coarse = width // STRIDE // 4, width // (2 * STRIDE) // 4
    fine_rows = fine * HALF
    fine_all = fine_rows + NYQ
    half_rows = fine_all + coarse * HALF
    levels = [(spec_fine, quads_fine, fine, 0, fine_rows, 0)]
    if coarse:
        levels.append((spec_coarse, quads_coarse, coarse, NYQ, 0, fine))

    for z in range(3):
        x = strips(z)
        t = dot(table_ref[row_at : row_at + 2 * half_rows, : 2 * x.shape[0]], jnp.concatenate([x, x], axis=0))
        for ref, half in zip((high_ref, low_ref), split(t)):
            ref[:, :width] = half
            ref[:, width:] = jnp.zeros((2 * half_rows, LANES), bf16)

        def windows(first, last, starts):
            result = []
            for ref in (high_ref, low_ref):
                pieces = []
                for tile in starts:
                    columns = []
                    for at in tile:
                        columns += [ref[first:last, at : at + LANES],
                                    ref[half_rows + first : half_rows + last, at : at + LANES]]
                    pieces.append(jnp.concatenate(columns, axis=1))
                result.append(jnp.concatenate(pieces, axis=0))
            return result

        starts = [[LANES * m + STRIDE * odd] for m in range(quads_fine) for odd in range(2)]
        f = dot3(*windows(0, fine_all, starts), table_ref, fine_at)
        for tile in range(len(starts)):
            spec_fine[z, tile] = f[tile * fine_all : (tile + 1) * fine_all]
        normalise(spec_fine, z, len(starts), fine, 0, fine_rows, 0)
        if coarse:
            starts = [[2 * LANES * n + LANES * p + 2 * STRIDE * odd for p in range(2)]
                      for n in range(quads_coarse) for odd in range(2)]
            f = dot3(*windows(fine_rows, half_rows, starts), table_ref, coarse_at)
            rows = half_rows - fine_rows
            for tile in range(len(starts)):
                spec_coarse[z, tile] = f[tile * rows : (tile + 1) * rows]
            normalise(spec_coarse, z, len(starts), coarse, NYQ, 0, fine)

    values = []
    for spec_ref, quads, blocks, first, nyquist, first_block in levels:
        for d in range(2):
            for quad in range(quads):
                columns = []
                for odd in range(2):
                    a, b = spec_ref[0, 2 * quad + odd], spec_ref[d + 1, 2 * quad + odd]
                    ar, ai, br, bi = a[:, :LANES], a[:, LANES:], b[:, :LANES], b[:, LANES:]
                    columns += [ar * br + ai * bi, ar * bi - ai * br]
                values.append(jnp.concatenate(columns, axis=1))
    y = dot3(*split(jnp.concatenate(values, axis=0)), table_ref, shift_at)

    starts = {}
    at = tile = 0
    for level, (spec_ref, quads, blocks, first, nyquist, first_block) in enumerate(levels):
        rows = blocks * HALF + NYQ
        for b in range(blocks):
            columns = []
            for i in range(2 * quads):
                top = at + i * rows + first + b * HALF
                nyq = at + i * rows + nyquist
                stack = jnp.concatenate(
                    [y[top : top + HALF, :LANES], y[top : top + HALF, LANES:], y[nyq : nyq + NYQ, :LANES]], axis=0)
                columns.append(jnp.concatenate(split(stack), axis=0))
            columns = jnp.concatenate(columns, axis=1)
            table = map_at + 2 * WINDOW * (first_block + b)
            both = dot(table_ref[table : table + 2 * WINDOW, : columns.shape[0]], columns)
            maps = both[:WINDOW] + both[WINDOW:]
            for i in range(2 * quads):
                maps_ref[tile + i] = maps[:, i * LANES : (i + 1) * LANES]
            for d in range(2):
                starts[level, d, b] = tile + d * quads
            tile += 2 * quads
        at += 2 * quads * rows

    kept = [jnp.transpose(mask) for mask in masks()]
    lanes = lax.broadcasted_iota(jnp.int32, (tile, LANES), 1) // WINDOW
    for big in range(WINDOW // 4):
        rows = [maps_ref[:, 4 * big + r, :] for r in range(4)]
        for g in range(4):
            value = None
            for r in range(4):
                moved = rows[r] if r == g else pltpu.roll(rows[r], (WINDOW * (r - g)) % LANES, 1)
                value = moved if value is None else jnp.where(lanes == r, moved, value)
            rows_ref[big, pl.ds(g, tile, stride=4), :] = value
        for level, out in enumerate(outs):
            quads, blocks = levels[level][1:3]
            for b in range(blocks):
                column = kept[level][: 4 * quads, b : b + 1]
                for d in range(2):
                    at = 4 * starts[level, d, b]
                    out[d, b, :, big * LANES : (big + 1) * LANES] = rows_ref[big, at : at + 4 * quads] * column


def mask_tile(mask_ref, pad_ref, first, count):
    pad_ref[...] = jnp.zeros(pad_ref.shape, f32)
    pad_ref[:count, : mask_ref.shape[2]] = mask_ref[0, first : first + count].astype(f32)
    return pad_ref[...]


def inner_kernel(
    fine, width, places,
    own_hbm, near, far, mask_hbm, table_hbm,
    out_hbm, table_ref,
    own, mask, pad, high_ref, low_ref, spec_fine, maps_ref, rows_ref, out, sems,
):
    own_copy = pltpu.make_async_copy(own_hbm, own, sems.at[0])
    mask_copy = pltpu.make_async_copy(mask_hbm, mask, sems.at[1])
    own_copy.start()
    mask_copy.start()
    row_at, fine_at, shift_at, map_at, coarse_at = places
    cuts = [0, fine_at, shift_at, coarse_at, table_hbm.shape[0]]
    copies = []
    for i in range(4):
        piece = pl.ds(cuts[i], cuts[i + 1] - cuts[i])
        copies.append(pltpu.make_async_copy(table_hbm.at[piece], table_ref.at[piece], sems.at[2 + i]))
        copies[-1].start()
    own_copy.wait()
    mask_copy.wait()
    for copy in copies:
        copy.wait()
    strips = (own, near, far)
    maps_of(
        fine, 0, width, lambda z: strips[z][0], lambda: [mask_tile(mask, pad, 0, fine)],
        table_ref, places, [out], (high_ref, low_ref, spec_fine, None, maps_ref, rows_ref))
    stores = [
        pltpu.make_async_copy(out.at[d], out_hbm.at[0, d, pl.ds(0, fine)], sems.at[d]) for d in range(2)]
    for store in stores:
        store.start()
    for store in stores:
        store.wait()


def outer_kernel(
    first, fine, coarse, width, places,
    own_hbm, near, far, rim, rim_near, rim_far, mask_hbm, mask_coarse_hbm, table_ref, part_hbm,
    out_hbm, out_coarse_hbm,
    own, mask, mask_coarse, pad, pad_coarse, high_ref, low_ref, spec_fine, spec_coarse, maps_ref, rows_ref,
    out, out_coarse, sems,
):
    loads = [
        pltpu.make_async_copy(own_hbm, own, sems.at[0]),
        pltpu.make_async_copy(mask_hbm, mask, sems.at[1]),
        pltpu.make_async_copy(mask_coarse_hbm, mask_coarse, sems.at[2]),
    ]
    for load in loads:
        load.start()
    for load in loads:
        load.wait()
    strips, rims = (own, near, far), (rim, rim_near, rim_far)
    maps_of(
        fine, coarse, width, lambda z: jnp.concatenate([strips[z][0], rims[z][0]], axis=0),
        lambda: [mask_tile(mask, pad, first, fine), mask_tile(mask_coarse, pad_coarse, 0, coarse)],
        table_ref, places, [out, out_coarse], (high_ref, low_ref, spec_fine, spec_coarse, maps_ref, rows_ref))
    stores = []
    for d in range(2):
        stores.append(pltpu.make_async_copy(out.at[d], out_hbm.at[0, d, pl.ds(first, fine)], sems.at[2 * d]))
        stores.append(pltpu.make_async_copy(out_coarse.at[d], out_coarse_hbm.at[0, d], sems.at[2 * d + 1]))
    for store in stores:
        store.start()
    for store in stores:
        store.wait()


def scratch_of(fine, coarse, width):
    quads_fine, quads_coarse = width // STRIDE // 4, width // (2 * STRIDE) // 4
    half_rows = (fine + coarse) * HALF + NYQ
    tiles = 2 * (fine * quads_fine + coarse * quads_coarse)
    shapes = [
        pltpu.VMEM((2 * half_rows, width + LANES), bf16),
        pltpu.VMEM((2 * half_rows, width + LANES), bf16),
        pltpu.VMEM((3, 2 * quads_fine, fine * HALF + NYQ, 2 * LANES), f32),
    ]
    if coarse:
        shapes.append(pltpu.VMEM((3, 2 * quads_coarse, coarse * HALF + NYQ, 2 * LANES), f32))
    shapes += [
        pltpu.VMEM((tiles, WINDOW, LANES), f32),
        pltpu.VMEM((WINDOW // 4, 4 * tiles, LANES), f32),
        pltpu.VMEM((2, fine, 4 * quads_fine, WINDOW * WINDOW), f32),
    ]
    if coarse:
        shapes.append(pltpu.VMEM((2, coarse, 4 * quads_coarse, WINDOW * WINDOW), f32))
    return shapes


def correlate(own, near, far, rims, mask_fine, mask_coarse):
    strip_rows, width = own.shape[1:]
    fine, coarse = mask_fine.shape[1], mask_coarse.shape[1]
    inner = fine - 1
    table, places = all_tables(
        strip_rows + PATCH, [(range(inner), []), (range(inner, fine), range(coarse))])
    ext = strip_rows + PATCH
    table[: places[1], strip_rows : 2 * strip_rows] = table[: places[1], ext : ext + strip_rows]
    row_in, row_out, fine_at, shift_at, map_at, coarse_at, _ = places
    hbm = pl.BlockSpec(memory_space=pltpu.HBM)
    vmem = pl.BlockSpec(memory_space=pltpu.VMEM)
    params = pltpu.CompilerParams(vmem_limit_bytes=24 * 1024 * 1024)
    out_fine = jax.ShapeDtypeStruct((1, 2, fine, width // STRIDE, WINDOW * WINDOW), f32)
    out_coarse = jax.ShapeDtypeStruct((1, 2, coarse, width // (2 * STRIDE), WINDOW * WINDOW), f32)

    part, tables = pl.pallas_call(
        functools.partial(inner_kernel, inner, width, (row_in, fine_at, shift_at, map_at, coarse_at)),
        out_shape=(out_fine, jax.ShapeDtypeStruct(table.shape, bf16)),
        in_specs=[hbm, vmem, vmem, hbm, hbm],
        out_specs=(hbm, vmem),
        scratch_shapes=[
            pltpu.VMEM(own.shape, bf16),
            pltpu.VMEM(mask_fine.shape, jnp.int32),
            pltpu.VMEM((8, LANES), f32),
            *scratch_of(inner, 0, width),
            pltpu.SemaphoreType.DMA((6,)),
        ],
        compiler_params=params,
        cost_estimate=pl.CostEstimate(flops=3 * 10**9, bytes_accessed=4 * 10**6, transcendentals=0),
        name="inner_blocks",
    )(own, near, far, mask_fine, jnp.asarray(table))
    return pl.pallas_call(
        functools.partial(
            outer_kernel, inner, fine - inner, coarse, width, (row_out, fine_at, shift_at, map_at, coarse_at)),
        out_shape=(out_fine, out_coarse),
        in_specs=[hbm, vmem, vmem, vmem, vmem, vmem, hbm, hbm, vmem, hbm],
        out_specs=(hbm, hbm),
        scratch_shapes=[
            pltpu.VMEM(own.shape, bf16),
            pltpu.VMEM(mask_fine.shape, jnp.int32),
            pltpu.VMEM(mask_coarse.shape, jnp.int32),
            pltpu.VMEM((8, LANES), f32),
            pltpu.VMEM((8, LANES), f32),
            *scratch_of(fine - inner, coarse, width),
            pltpu.SemaphoreType.DMA((4,)),
        ],
        input_output_aliases={9: 0},
        compiler_params=params,
        cost_estimate=pl.CostEstimate(flops=4 * 10**9, bytes_accessed=4 * 10**6, transcendentals=0),
        name="outer_blocks",
    )(own, near, far, *rims, mask_fine, mask_coarse, tables, part)


def local(sections, mask_fine, mask_coarse):
    far = from_device(sections, 2, 0)
    near = from_device(sections, 1, 0)
    rims = [from_device(sections, 0, 1), from_device(sections, 1, 1), from_device(sections, 2, 1)]
    return correlate(sections, near, far, rims, mask_fine, mask_coarse)


def solution(mesh):
    in_specs = (
        P("sec", "strip", "groups"),
        P("sec", "strip", "groups"),
        P("sec", "strip", "groups"),
    )
    out_specs = (P("sec", None, "strip", "groups", None), P("sec", None, "strip", "groups", None))
    return jax.shard_map(local, mesh=mesh, in_specs=in_specs, out_specs=out_specs, check_vma=False)
```

time: 28.3 us -> 23.1 us (0.82)
  the two profiles are of different devices: /device:TPU:1 before, /device:TPU:19 now
where the time goes in v2:
time: 23.1 us; the launch traced here: 22.8 us
  starting transfers between devices  9.96 us (43%)
  Pallas kernels  9.24 us (40%)
  local copies, waits for them, and re-layouts  2.9 us (13%)
  between operations  0.74 us (3%)
    ppermute x5, starting transfers between devices, from_device(): return lax.ppermute(value, ('sec', 'strip'), pairs)  9.96 us
    pallas_call x1, Pallas kernels, correlate(): pl.pallas_call(functools.partial(outer_kernel, inner, fine - inner, coars...  5.13 us
    pallas_call x1, Pallas kernels, correlate(): pl.pallas_call(functools.partial(inner_kernel, inner, width, (row_in, fin...  4.11 us
    unnamed x8, local copies, waits for them, and re-layouts  2.9 us
  transfers between devices with their start and end apart: 5, of which 0 were waited for; matrix products, arithmetic and copies ran while one was open for 0% of the time, Pallas kernels for 18%

profile of v2, /device:TPU:19, one launch (start us, length us, event | category | flops | bytes accessed | tf_op | source)
XLA Modules:
  0.0 22.8 jit_solution(5794502321726225403)
XLA Ops:
  0.6 2.0 %collective-permute-start.1 = (bf16[1,64,512]{2,1,0:T(8,128)(2,1)}, bf16[1,64,512]{2,1,0:T(8,128)(2,1)S(1)}, u32[]{:S(2)}, u32[]{:S(2)}) collective-permute-start(bf16[1,64,512]{2,1,0:T(8,128)(2,1)} %own_hbm.3), channel_id=1, source_target_pairs={{8,0},{9,1},{10,2},{11,3},{12,4},{13,5},{14,6},{15,7},{24,16},{25,... | collective-permute-start | bytes 196616 | tf_op jit(solution)/shard_map/ppermute | solution.py:28
  2.6 1.9 %collective-permute-start = (bf16[1,64,512]{2,1,0:T(8,128)(2,1)}, bf16[1,64,512]{2,1,0:T(8,128)(2,1)S(1)}, u32[]{:S(2)}, u32[]{:S(2)}) collective-permute-start(bf16[1,64,512]{2,1,0:T(8,128)(2,1)} %own_hbm.3), channel_id=1, source_target_pairs={{4,0},{5,1},{6,2},{7,3},{8,4},{9,5},{10,6},{11,7},{12,8},{13,9},{1... | collective-permute-start | bytes 196616 | tf_op jit(solution)/shard_map/ppermute | solution.py:28
  4.5 1.3 %collective-permute-start.4 = (bf16[1,64,512]{2,1,0:T(8,128)(2,1)}, bf16[1,64,512]{2,1,0:T(8,128)(2,1)S(1)}, u32[]{:S(2)}, u32[]{:S(2)}) collective-permute-start(bf16[1,64,512]{2,1,0:T(8,128)(2,1)} %own_hbm.3), channel_id=1, source_target_pairs={{9,0},{10,1},{11,2},{13,4},{14,5},{15,6},{25,16},{26,17},{27,18},{... | collective-permute-start | bytes 196616 | tf_op jit(solution)/shard_map/ppermute | solution.py:28
  5.8 2.4 %collective-permute-start.3 = (bf16[1,64,512]{2,1,0:T(8,128)(2,1)}, bf16[1,64,512]{2,1,0:T(8,128)(2,1)S(1)}, u32[]{:S(2)}, u32[]{:S(2)}) collective-permute-start(bf16[1,64,512]{2,1,0:T(8,128)(2,1)} %own_hbm.3), channel_id=1, source_target_pairs={{5,0},{6,1},{7,2},{9,4},{10,5},{11,6},{13,8},{14,9},{15,10},{21,16... | collective-permute-start | bytes 196616 | tf_op jit(solution)/shard_map/ppermute | solution.py:28
  8.2 2.4 %collective-permute-start.2 = (bf16[1,64,512]{2,1,0:T(8,128)(2,1)}, bf16[1,64,512]{2,1,0:T(8,128)(2,1)S(1)}, u32[]{:S(2)}, u32[]{:S(2)}) collective-permute-start(bf16[1,64,512]{2,1,0:T(8,128)(2,1)} %own_hbm.3), channel_id=1, source_target_pairs={{1,0},{2,1},{3,2},{5,4},{6,5},{7,6},{9,8},{10,9},{11,10},{13,12},{... | collective-permute-start | bytes 196616 | tf_op jit(solution)/shard_map/ppermute | solution.py:28
  10.6 0.0 collective-permute-done.1.far
  10.6 0.0 collective-permute-done.near
  10.6 0.0 copy-start
  10.7 0.8 %copy-done = bf16[1,64,512]{2,1,0:T(8,128)(2,1)S(1)} copy-done((bf16[1,64,512]{2,1,0:T(8,128)(2,1)S(1)}, bf16[1,64,512]{2,1,0:T(8,128)(2,1)}, u32[]{:S(2)}) %copy-start) | copy-done | bytes 65560
  11.5 0.0 copy-start.1
  11.5 0.7 %copy-done.1 = s32[1,2,16]{2,1,0:T(2,128)S(1)} copy-done((s32[1,2,16]{2,1,0:T(2,128)S(1)}, s32[1,2,16]{2,1,0:T(2,128)}, u32[]{:S(2)}) %copy-start.1) | copy-done | bytes 152
  12.2 0.0 copy-start.3
  12.2 1.4 %copy-done.3 = bf16[2944,256]{1,0:T(8,128)(2,1)S(1)} copy-done((bf16[2944,256]{1,0:T(8,128)(2,1)S(1)}, bf16[2944,256]{1,0:T(8,128)(2,1)}, u32[]{:S(2)}) %copy-start.3) | copy-done | bytes 1507352
  13.6 0.0 copy-start.2
  13.6 4.1 %inner_blocks.1 = (f32[1,2,2,16,1024]{4,3,2,1,0:T(8,128)}, bf16[2944,256]{1,0:T(8,128)(2,1)S(1)}) custom-call(bf16[1,64,512]{2,1,0:T(8,128)(2,1)S(1)} %copy-done, bf16[1,64,512]{2,1,0:T(8,128)(2,1)S(1)} %collective-permute-done.near, bf16[1,64,512]{2,1,0:T(8,128)(2,1)S(1)} %collective-permute-done.1.far, s32[1,2,16]{2,1,0:T(2,128)S(1)} %copy-done.1, ...), custom_call_target="tpu_custom_call" | custom-call | flops 3000000000 | bytes 4000000 | tf_op jit(solution)/shard_map/inner_blocks/pallas_call | solution.py:398
  17.7 0.0 collective-permute-done.4.rim_far
  17.7 0.0 collective-permute-done.3.rim_near
  17.7 0.0 collective-permute-done.2.rim
  17.7 0.0 copy-done.2
  17.7 5.1 %outer_blocks.1 = (f32[1,2,2,16,1024]{4,3,2,1,0:T(8,128)}, f32[1,2,1,8,1024]{4,3,2,1,0:T(8,128)}) custom-call(bf16[1,64,512]{2,1,0:T(8,128)(2,1)S(1)} %copy-done, bf16[1,64,512]{2,1,0:T(8,128)(2,1)S(1)} %collective-permute-done.near, bf16[1,64,512]{2,1,0:T(8,128)(2,1)S(1)} %collective-permute-done.1.far, ...), custom_call_target="tpu_custom_call", output_to_operand_aliasing={{0}: (9, {})} | custom-call | flops 4000000000 | bytes 4000000 | tf_op jit(solution)/shard_map/outer_blocks/pallas_call | solution.py:414
Async XLA Ops:
  0.6 10.0 %collective-permute-start.1 = (bf16[1,64,512]{2,1,0:T(8,128)(2,1)}, bf16[1,64,512]{2,1,0:T(8,128)(2,1)S(1)}, u32[]{:S(2)}, u32[]{:S(2)}) collective-permute-start(bf16[1,64,512]{2,1,0:T(8,128)(2,1)} %own_hbm.3), channel_id=1, source_target_pairs={{8,0},{9,1},{10,2},{11,3},{12,4},{13,5},{14,6},{15,7},{24,16},{25,... | collective-permute-start | bytes 196616 | tf_op jit(solution)/shard_map/ppermute | solution.py:28
  2.6 8.0 %collective-permute-start = (bf16[1,64,512]{2,1,0:T(8,128)(2,1)}, bf16[1,64,512]{2,1,0:T(8,128)(2,1)S(1)}, u32[]{:S(2)}, u32[]{:S(2)}) collective-permute-start(bf16[1,64,512]{2,1,0:T(8,128)(2,1)} %own_hbm.3), channel_id=1, source_target_pairs={{4,0},{5,1},{6,2},{7,3},{8,4},{9,5},{10,6},{11,7},{12,8},{13,9},{1... | collective-permute-start | bytes 196616 | tf_op jit(solution)/shard_map/ppermute | solution.py:28
  4.5 13.1 %collective-permute-start.4 = (bf16[1,64,512]{2,1,0:T(8,128)(2,1)}, bf16[1,64,512]{2,1,0:T(8,128)(2,1)S(1)}, u32[]{:S(2)}, u32[]{:S(2)}) collective-permute-start(bf16[1,64,512]{2,1,0:T(8,128)(2,1)} %own_hbm.3), channel_id=1, source_target_pairs={{9,0},{10,1},{11,2},{13,4},{14,5},{15,6},{25,16},{26,17},{27,18},{... | collective-permute-start | bytes 196616 | tf_op jit(solution)/shard_map/ppermute | solution.py:28
  5.8 11.9 %collective-permute-start.3 = (bf16[1,64,512]{2,1,0:T(8,128)(2,1)}, bf16[1,64,512]{2,1,0:T(8,128)(2,1)S(1)}, u32[]{:S(2)}, u32[]{:S(2)}) collective-permute-start(bf16[1,64,512]{2,1,0:T(8,128)(2,1)} %own_hbm.3), channel_id=1, source_target_pairs={{5,0},{6,1},{7,2},{9,4},{10,5},{11,6},{13,8},{14,9},{15,10},{21,16... | collective-permute-start | bytes 196616 | tf_op jit(solution)/shard_map/ppermute | solution.py:28
  8.2 9.5 %collective-permute-start.2 = (bf16[1,64,512]{2,1,0:T(8,128)(2,1)}, bf16[1,64,512]{2,1,0:T(8,128)(2,1)S(1)}, u32[]{:S(2)}, u32[]{:S(2)}) collective-permute-start(bf16[1,64,512]{2,1,0:T(8,128)(2,1)} %own_hbm.3), channel_id=1, source_target_pairs={{1,0},{2,1},{3,2},{5,4},{6,5},{7,6},{9,8},{10,9},{11,10},{13,12},{... | collective-permute-start | bytes 196616 | tf_op jit(solution)/shard_map/ppermute | solution.py:28
  10.6 0.8 %copy-start = (bf16[1,64,512]{2,1,0:T(8,128)(2,1)S(1)}, bf16[1,64,512]{2,1,0:T(8,128)(2,1)}, u32[]{:S(2)}) copy-start(bf16[1,64,512]{2,1,0:T(8,128)(2,1)} %own_hbm.3) | copy-start | bytes 196612
  11.5 0.7 %copy-start.1 = (s32[1,2,16]{2,1,0:T(2,128)S(1)}, s32[1,2,16]{2,1,0:T(2,128)}, u32[]{:S(2)}) copy-start(s32[1,2,16]{2,1,0:T(2,128)} %mask_hbm.3) | copy-start | bytes 388
  12.2 1.4 %copy-start.3 = (bf16[2944,256]{1,0:T(8,128)(2,1)S(1)}, bf16[2944,256]{1,0:T(8,128)(2,1)}, u32[]{:S(2)}) copy-start(bf16[2944,256]{1,0:T(8,128)(2,1)} %constant.2.clone.table_hbm) | copy-start | bytes 4521988
  13.6 4.2 %copy-start.2 = (s32[1,1,8]{2,1,0:T(1,128)S(1)}, s32[1,1,8]{2,1,0:T(1,128)}, u32[]{:S(2)}) copy-start(s32[1,1,8]{2,1,0:T(1,128)} %mask_coarse_hbm.1) | copy-start | bytes 100
